TPU v7x, 256 devices: a whole 4x4x8 slice. The times are simulated.
256 devices in a mesh: row: 8 (over y_hi, x), col: 32 (over y_lo, z, core).
Axes of the slice: x: 4, y: 4 (y_hi: 2, y_lo: 2; y = y_hi * 2 + y_lo), z: 8, core: 2. Of those that a mesh axis runs over, the one named last changes fastest.
Arguments:
- pair_rep: bfloat16 [128, 2048, 128], P('row', 'col'), may hold values from -6 to 6
- w_proj: bfloat16 [128, 512], replicated, may hold values from -0.5 to 0.5
- bias_logits: bfloat16 [4, 2048, 2048], P(None, 'row', 'col'), may hold values from -6 to 400
- chain_lengths: int32 [4], replicated, may hold values from 1 to 512, 1536 in all
- w_out: bfloat16 [128, 128], replicated, may hold values from -0.5 to 0.5
- grad_out: bfloat16 [128, 2048, 128], P('row', 'col'), may hold values from -96 to 96
Outputs:
- pair_grad: bfloat16 [128, 2048, 128], P('row', 'col')
- bias_grad: float32 [4, 2048, 2048], P(None, 'row', 'col')
- proj_grad: float32 [128, 512], replicated
- out_grad: float32 [128, 128], replicated
All inputs are finite; a program needn't handle non-finite values.
Results may differ from a plain program's by a relative error of at most 0.015.
Values may be sent and summed in bfloat16 or wider, within the bound.
No kernel may reach another device: no remote copies, remote signals or barrier semaphores. Data moves between devices by JAX's collectives and lax.ppermute only.
A program may use at most 128 MiB of HBM per device.

v0:
```python
import math

import jax
import jax.numpy as jnp
from jax import lax
from jax.sharding import PartitionSpec as P

H = 4
D = 32
CHAINS = 4


NEG_BIG = -1e30


def key_valid(chain_lengths, length_total):
    slot_count = length_total // CHAINS
    position = jnp.arange(length_total, dtype=jnp.int32)
    chain_of = position // slot_count
    chain_ids = jnp.arange(CHAINS, dtype=jnp.int32)
    chain_limit = jnp.sum(
        jnp.where(chain_of[:, None] == chain_ids[None, :], chain_lengths[None, :], 0), axis=1
    )
    return position % slot_count < chain_limit


def on_device(pair_rep, w_proj, bias_logits, chain_lengths, w_out, grad_out):
    col_count = lax.axis_size("col")
    group_size = col_count // H
    head_index = lax.axis_index("col") // group_size
    rows_dev, cols_dev, channels = pair_rep.shape
    sub_rows = rows_dev // group_size
    full_len = cols_dev * col_count
    width_head = 4 * D
    score_scale = D ** (-0.5)
    key_mask = key_valid(chain_lengths, full_len)
    block_rows = math.gcd(512, full_len)
    block_count = full_len // block_rows
    bias_rows = lax.all_gather(bias_logits, "row", axis=1, tiled=True)
    copies = jnp.repeat(bias_rows, group_size, axis=0)
    bias_head = lax.all_to_all(copies, "col", split_axis=0, concat_axis=2, tiled=True)[0]
    bias_blocks = bias_head.reshape(block_count, block_rows, full_len)
    w_head = lax.dynamic_slice_in_dim(w_proj, head_index * width_head, width_head, 1)
    w_out_head = lax.dynamic_slice_in_dim(w_out, head_index * D, D, 0)

    def spread(source_block):
        return jnp.tile(source_block.reshape(group_size, sub_rows, cols_dev * channels), (H, 1, 1))

    pair_rows, grad_rows = (
        lax.all_to_all(spread(pair_rep), "col", split_axis=0, concat_axis=2, tiled=True),
        lax.all_to_all(spread(grad_out), "col", split_axis=0, concat_axis=2, tiled=True),
    )
    pair_rows = pair_rows.reshape(sub_rows, full_len, channels)
    grad_rows = grad_rows.reshape(sub_rows, full_len, channels)
    proj_head = jnp.dot(pair_rows, w_head, preferred_element_type=jnp.float32).astype(jnp.bfloat16)
    ograd_head = jnp.dot(grad_rows, w_out_head.T, preferred_element_type=jnp.float32).astype(
        jnp.bfloat16
    )
    block_starts = jnp.arange(block_count, dtype=jnp.int32) * block_rows

    def attend(bias_acc, inputs):
        proj_row, ograd_row = inputs
        queries = proj_row[:, :D]
        keys_row = proj_row[:, D : 2 * D]
        values_row = proj_row[:, 2 * D : 3 * D]
        gates_row = proj_row[:, 3 * D :]

        def block_step(carry, block_in):
            acc, key_acc, value_acc = carry
            start, query_blk, gate_blk, ograd_blk, bias_blk = block_in
            scores = jnp.dot(
                query_blk, keys_row.T, preferred_element_type=jnp.float32
            ) * score_scale + bias_blk.astype(jnp.float32)
            scores = jnp.where(key_mask[None, :], scores, NEG_BIG)
            row_max = jnp.max(scores, axis=1, keepdims=True)
            exp_scores = jnp.exp(scores - row_max)
            attn_prob = exp_scores / jnp.sum(exp_scores, axis=1, keepdims=True)
            prob_half = attn_prob.astype(jnp.bfloat16)
            attended = jnp.dot(prob_half, values_row, preferred_element_type=jnp.float32)
            gate_sig = jax.nn.sigmoid(gate_blk.astype(jnp.float32))
            gated = (gate_sig * attended).astype(jnp.bfloat16)
            ograd = ograd_blk.astype(jnp.float32)
            attn_grad = (ograd * gate_sig).astype(jnp.bfloat16)
            gate_grad = ograd * attended * gate_sig * (1.0 - gate_sig)
            value_part = jnp.dot(prob_half.T, attn_grad, preferred_element_type=jnp.float32)
            prob_grad = jnp.dot(attn_grad, values_row.T, preferred_element_type=jnp.float32)
            delta_row = jnp.sum(attn_grad.astype(jnp.float32) * attended, axis=1, keepdims=True)
            score_grad = attn_prob * (prob_grad - delta_row)
            score_half = score_grad.astype(jnp.bfloat16)
            query_grad = (
                jnp.dot(score_half, keys_row, preferred_element_type=jnp.float32) * score_scale
            )
            key_part = (
                jnp.dot(score_half.T, query_blk, preferred_element_type=jnp.float32) * score_scale
            )
            previous = lax.dynamic_slice_in_dim(acc, start, block_rows, 0)
            acc = lax.dynamic_update_slice_in_dim(acc, previous + score_grad, start, 0)
            return (
                (acc, key_acc + key_part, value_acc + value_part),
                (query_grad, gate_grad, gated),
            )

        empty = jnp.zeros((full_len, D), jnp.float32)
        (bias_acc, key_grad, value_grad), (query_grad, gate_grad, gated) = lax.scan(
            block_step,
            (bias_acc, empty, empty),
            (
                block_starts,
                queries.reshape(block_count, block_rows, D),
                gates_row.reshape(block_count, block_rows, D),
                ograd_row.reshape(block_count, block_rows, D),
                bias_blocks,
            ),
        )
        query_grad = query_grad.reshape(full_len, D)
        gate_grad = gate_grad.reshape(full_len, D)
        proj_row_grad = jnp.concatenate(
            [query_grad, key_grad, value_grad, gate_grad], axis=1
        ).astype(jnp.bfloat16)
        return (bias_acc, (proj_row_grad, gated.reshape(full_len, D)))

    bias_part, (proj_grads_head, gated_head) = lax.scan(
        attend, jnp.zeros((full_len, full_len), jnp.float32), (proj_head, ograd_head)
    )
    partial_pair = jnp.dot(proj_grads_head, w_head.T, preferred_element_type=jnp.float32)
    returned = lax.all_to_all(
        partial_pair.reshape(sub_rows, full_len * channels),
        "col",
        split_axis=1,
        concat_axis=0,
        tiled=True,
    )
    summed = jnp.sum(returned.reshape(H, group_size, sub_rows, cols_dev, channels), axis=0)
    pair_grad = summed.reshape(rows_dev, cols_dev, channels).astype(jnp.bfloat16)
    proj_part = jnp.dot(
        pair_rows.reshape(-1, channels).T,
        proj_grads_head.reshape(-1, width_head),
        preferred_element_type=jnp.float32,
    )
    proj_local = lax.dynamic_update_slice_in_dim(
        jnp.zeros((channels, 4 * H * D), jnp.float32), proj_part, head_index * width_head, 1
    )
    out_part = jnp.dot(
        gated_head.reshape(-1, D).T,
        grad_rows.reshape(-1, channels),
        preferred_element_type=jnp.float32,
    )
    out_local = lax.dynamic_update_slice_in_dim(
        jnp.zeros((H * D, channels), jnp.float32), out_part, head_index * D, 0
    )
    proj_grad, out_grad = lax.psum((proj_local / full_len, out_local / full_len), ("row", "col"))
    bias_share = lax.psum_scatter(bias_part, "row", scatter_dimension=0, tiled=True)
    bias_pieces = lax.all_to_all(bias_share[None], "col", split_axis=2, concat_axis=0, tiled=True)
    bias_grad = jnp.sum(bias_pieces.reshape(H, group_size, bias_share.shape[0], cols_dev), axis=1)
    return (pair_grad, bias_grad, proj_grad, out_grad)


def solution(mesh):
    return jax.shard_map(
        on_device,
        mesh=mesh,
        in_specs=(
            P("row", "col", None),
            P(),
            P(None, "row", "col"),
            P(),
            P(),
            P("row", "col", None),
        ),
        out_specs=(P("row", "col", None), P(None, "row", "col"), P(), P()),
        check_vma=False,
    )
```

profile of v0, /device:TPU:1, one launch (start us, length us, event | category | flops | bytes accessed | tf_op | source)
XLA Modules:
  0.0 1106.8 jit_solution(11000200875969801250)
XLA Ops:
  8.2 2.0 tile.24
  10.2 11.1 %all-to-all-start.1 = ((bf16[32,2,8192]{2,1,0:T(2,128)(2,1)}), bf16[32,2,8192]{2,1,0:T(2,128)(2,1)S(1)}, u32[]{:S(2)}, u32[]{:S(2)}) async-start(bf16[32,2,8192]{2,1,0:T(2,128)(2,1)} %bitcast.6), calls=%async_computation.1 | async-start | bytes 2097152 | tf_op jit(solution)/shard_map/all_to_all | solution.py:51
  22.4 25.4 %all-to-all-done.1 = bf16[32,2,8192]{2,1,0:T(2,128)(2,1)S(1)} async-done(((bf16[32,2,8192]{2,1,0:T(2,128)(2,1)}), bf16[32,2,8192]{2,1,0:T(2,128)(2,1)S(1)}, u32[]{:S(2)}, u32[]{:S(2)}) %all-to-all-start.1) | async-done | bytes 1048608 | tf_op jit(solution)/shard_map/all_to_all | solution.py:51
  47.8 2.0 tile.21
  49.8 6.0 all-to-all-start
  56.5 55.3 %all-gather.2.cloned.1.call-done = bf16[4,2048,64]{1,2,0:T(8,128)(2,1)} async-done(((bf16[4,256,64]{1,2,0:T(8,128)(2,1)}), bf16[4,2048,64]{1,2,0:T(8,128)(2,1)}) %all-gather.2.cloned.1.call-update) | async-done | bytes 1048592 | tf_op jit(solution)/shard_map/all_gather | solution.py:39
  111.8 5.5 broadcast_in_dim.74
  117.4 9.4 all-to-all-start.2
  130.3 2.4 fusion.30
  133.1 177.7 %all-to-all-done.2 = bf16[32,2048,64]{1,2,0:T(8,128)(2,1)} async-done(((bf16[32,2048,64]{1,2,0:T(8,128)(2,1)}), bf16[32,2048,64]{1,2,0:T(8,128)(2,1)}, u32[]{:S(2)}, u32[]{:S(2)}) %all-to-all-start.2) | async-done | bytes 8388640 | tf_op jit(solution)/shard_map/all_to_all | solution.py:41
  310.9 14.6 %reshape_squeeze.3 = bf16[4,512,2048]{1,0,2:T(4,128)(2,1)} reshape(bf16[1,2048,32,64]{1,3,2,0:T(8,128)(2,1)} %bitcast.12) | data formatting | bytes 16777216 | tf_op jit(solution)/shard_map/reshape;squeeze | solution.py:42
  325.4 13.7 %copy.87 = bf16[4,512,2048]{2,1,0:T(8,128)(2,1)} copy(bf16[4,512,2048]{1,0,2:T(4,128)(2,1)} %reshape_squeeze.3) | data formatting | bytes 16777216
  339.2 7.9 broadcast_in_dim.69
  347.0 239.6 %while.38 = (s32[]{:T(128)}, f32[2048,2048]{1,0:T(8,128)}, bf16[2,2048,128]{1,2,0:T(8,128)(2,1)}, bf16[2,2048,32]{2,1,0:T(8,128)(2,1)}, bf16[2,2048,128]{1,2,0:T...) while((s32[]{:T(128)}, f32[2048,2048]{1,0:T(8,128)}, ...), condition=%wide.region_7.8_spmd.clone, body=%wide.region_1.7_spmd.clone.sunk | while | flops 421591552 | bytes 83642088 | solution.py:122
  349.3 112.2 %while.39 = (s32[]{:T(128)}, f32[2048,2048]{1,0:T(8,128)}, f32[2048,32]{0,1:T(8,128)S(1)}, f32[2048,32]{0,1:T(8,128)S(1)}, bf16[4,512,32]{1,2,0:T(8,128)(2,1)}, ...) while((s32[]{:T(128)}, f32[2048,2048]{1,0:T(8,128)}, ...), condition=%wide.region_6.6_spmd.clone, body=%wide.region_2.5_spmd.clone.sunk | while | flops 419363328 | bytes 58869056 | solution.py:104
  351.6 2.6 fusion.89
  358.3 5.5 dynamic-slice_add_fusion.2
  363.8 1.3 fusion.93
  365.6 11.8 %dynamic_update_slice.54 = f32[2048,2048]{1,0:T(8,128)} dynamic-update-slice(f32[2048,2048]{1,0:T(8,128)} %get-tuple-element.613, f32[512,2048]{1,0:T(8,128)} %get-tuple-element.591, s32[]{:T(128)S(6)} %select_n.55, s32[]{:T(128)} %constant.103.clone.1..sunk.1..sunk) | dynamic-update-slice | bytes 8388612 | tf_op jit(solution)/shard_map/while/body/eval_jaxpr/while/body/eval_jaxpr/dynamic_update_slice | solution.py:97
  379.7 2.6 fusion.89
  386.5 5.5 dynamic-slice_add_fusion.2
  391.9 1.3 fusion.93
  393.8 11.8 %dynamic_update_slice.54 = f32[2048,2048]{1,0:T(8,128)} dynamic-update-slice(f32[2048,2048]{1,0:T(8,128)} %get-tuple-element.613, f32[512,2048]{1,0:T(8,128)} %get-tuple-element.591, s32[]{:T(128)S(6)} %select_n.55, s32[]{:T(128)} %constant.103.clone.1..sunk.1..sunk) | dynamic-update-slice | bytes 8388612 | tf_op jit(solution)/shard_map/while/body/eval_jaxpr/while/body/eval_jaxpr/dynamic_update_slice | solution.py:97
  407.9 2.6 fusion.89
  414.7 5.5 dynamic-slice_add_fusion.2
  420.1 1.3 fusion.93
  422.0 11.9 %dynamic_update_slice.54 = f32[2048,2048]{1,0:T(8,128)} dynamic-update-slice(f32[2048,2048]{1,0:T(8,128)} %get-tuple-element.613, f32[512,2048]{1,0:T(8,128)} %get-tuple-element.591, s32[]{:T(128)S(6)} %select_n.55, s32[]{:T(128)} %constant.103.clone.1..sunk.1..sunk) | dynamic-update-slice | bytes 8388612 | tf_op jit(solution)/shard_map/while/body/eval_jaxpr/while/body/eval_jaxpr/dynamic_update_slice | solution.py:97
  436.1 2.6 fusion.89
  442.9 5.5 dynamic-slice_add_fusion.2
  448.3 1.3 fusion.93
  450.2 11.3 %dynamic_update_slice.54 = f32[2048,2048]{1,0:T(8,128)} dynamic-update-slice(f32[2048,2048]{1,0:T(8,128)} %get-tuple-element.613, f32[512,2048]{1,0:T(8,128)} %get-tuple-element.591, s32[]{:T(128)S(6)} %select_n.55, s32[]{:T(128)} %constant.103.clone.1..sunk.1..sunk) | dynamic-update-slice | bytes 8388612 | tf_op jit(solution)/shard_map/while/body/eval_jaxpr/while/body/eval_jaxpr/dynamic_update_slice | solution.py:97
  469.1 112.2 %while.39 = (s32[]{:T(128)}, f32[2048,2048]{1,0:T(8,128)}, f32[2048,32]{0,1:T(8,128)S(1)}, f32[2048,32]{0,1:T(8,128)S(1)}, bf16[4,512,32]{1,2,0:T(8,128)(2,1)}, ...) while((s32[]{:T(128)}, f32[2048,2048]{1,0:T(8,128)}, ...), condition=%wide.region_6.6_spmd.clone, body=%wide.region_2.5_spmd.clone.sunk | while | flops 419363328 | bytes 58869056 | solution.py:104
  471.4 2.6 fusion.89
  478.1 5.5 dynamic-slice_add_fusion.2
  483.6 1.3 fusion.93
  485.4 11.8 %dynamic_update_slice.54 = f32[2048,2048]{1,0:T(8,128)} dynamic-update-slice(f32[2048,2048]{1,0:T(8,128)} %get-tuple-element.613, f32[512,2048]{1,0:T(8,128)} %get-tuple-element.591, s32[]{:T(128)S(6)} %select_n.55, s32[]{:T(128)} %constant.103.clone.1..sunk.1..sunk) | dynamic-update-slice | bytes 8388612 | tf_op jit(solution)/shard_map/while/body/eval_jaxpr/while/body/eval_jaxpr/dynamic_update_slice | solution.py:97
  499.6 2.6 fusion.89
  506.3 5.5 dynamic-slice_add_fusion.2
  511.8 1.3 fusion.93
  513.6 11.8 %dynamic_update_slice.54 = f32[2048,2048]{1,0:T(8,128)} dynamic-update-slice(f32[2048,2048]{1,0:T(8,128)} %get-tuple-element.613, f32[512,2048]{1,0:T(8,128)} %get-tuple-element.591, s32[]{:T(128)S(6)} %select_n.55, s32[]{:T(128)} %constant.103.clone.1..sunk.1..sunk) | dynamic-update-slice | bytes 8388612 | tf_op jit(solution)/shard_map/while/body/eval_jaxpr/while/body/eval_jaxpr/dynamic_update_slice | solution.py:97
  527.7 2.6 fusion.89
  534.5 5.5 dynamic-slice_add_fusion.2
  539.9 1.3 fusion.93
  541.8 11.9 %dynamic_update_slice.54 = f32[2048,2048]{1,0:T(8,128)} dynamic-update-slice(f32[2048,2048]{1,0:T(8,128)} %get-tuple-element.613, f32[512,2048]{1,0:T(8,128)} %get-tuple-element.591, s32[]{:T(128)S(6)} %select_n.55, s32[]{:T(128)} %constant.103.clone.1..sunk.1..sunk) | dynamic-update-slice | bytes 8388612 | tf_op jit(solution)/shard_map/while/body/eval_jaxpr/while/body/eval_jaxpr/dynamic_update_slice | solution.py:97
  555.9 2.6 fusion.89
  562.7 5.5 dynamic-slice_add_fusion.2
  568.1 1.3 fusion.93
  570.0 11.3 %dynamic_update_slice.54 = f32[2048,2048]{1,0:T(8,128)} dynamic-update-slice(f32[2048,2048]{1,0:T(8,128)} %get-tuple-element.613, f32[512,2048]{1,0:T(8,128)} %get-tuple-element.591, s32[]{:T(128)S(6)} %select_n.55, s32[]{:T(128)} %constant.103.clone.1..sunk.1..sunk) | dynamic-update-slice | bytes 8388612 | tf_op jit(solution)/shard_map/while/body/eval_jaxpr/while/body/eval_jaxpr/dynamic_update_slice | solution.py:97
  586.7 17.6 %copy.93 = f32[2048,2048]{0,1:T(8,128)} copy(f32[2048,2048]{1,0:T(8,128)} %get-tuple-element.136) | data formatting | bytes 33554432 | tf_op jit(solution)/shard_map/while | solution.py:122
  605.5 1.8 fusion.31
  607.3 2.0 all_to_all.65
  609.3 3.0 copy.90
  612.2 10.3 all-to-all-start.3
  622.6 199.1 %reduce-scatter.2.cloned.1.call-done = f32[256,2048]{0,1:T(8,128)} async-done(((f32[2048,2048]{0,1:T(8,128)}), f32[256,2048]{0,1:T(8,128)}) %reduce-scatter.2.cloned.1.call-update) | async-done | bytes 2097168 | tf_op jit(solution)/shard_map/reduce_scatter | solution.py:152
  821.7 4.4 broadcast_in_dim.75
  826.2 11.5 %all-to-all-start.4 = ((f32[1,256,2048]{1,0,2:T(1,128)}), f32[1,256,2048]{1,0,2:T(1,128)}, u32[]{:S(2)}, u32[]{:S(2)}) async-start(f32[1,256,2048]{1,0,2:T(1,128)} %broadcast_in_dim.75), calls=%async_computation.5 | async-start | bytes 4194304 | tf_op jit(solution)/shard_map/all_to_all | solution.py:153
  840.2 1.7 convolution_bitcast_fusion
  842.1 1.6 convolution_dynamic-update-slice_fusion
  845.1 3.1 reshape.156
  849.3 38.5 %all-to-all-done.4 = f32[1,256,2048]{1,0,2:T(1,128)} async-done(((f32[1,256,2048]{1,0,2:T(1,128)}), f32[1,256,2048]{1,0,2:T(1,128)}, u32[]{:S(2)}, u32[]{:S(2)}) %all-to-all-start.4) | async-done | bytes 2097184 | tf_op jit(solution)/shard_map/all_to_all | solution.py:153
  887.8 1.7 copy.104
  890.4 206.8 %all-reduce.3.cloned.1.call-done = (f32[128,512]{1,0:T(8,128)}, f32[128,128]{1,0:T(8,128)}) async-done(((f32[128,512]{1,0:T(8,128)}, f32[128,128]{1,0:T(8,128)}), (f32[128,512]{1,0:T(8,128)}, f32[128,128]{1,0:T(8,128)})) %all-reduce.3.cloned.1.call-update) | async-done | bytes 327696 | tf_op jit(solution)/shard_map/psum | solution.py:151
  1097.1 1.7 copy.166
  1098.8 1.5 copy.167
  (201 shorter events, 70.1 us)
Async XLA Ops:
  7.2 125.5 %copy-start = (bf16[128,512]{1,0:T(8,128)(2,1)S(1)}, bf16[128,512]{1,0:T(8,128)(2,1)}, u32[]{:S(2)}) copy-start(bf16[128,512]{1,0:T(8,128)(2,1)} %param.11) | copy-start | bytes 393220
  10.2 37.6 %all-to-all-start.1 = ((bf16[32,2,8192]{2,1,0:T(2,128)(2,1)}), bf16[32,2,8192]{2,1,0:T(2,128)(2,1)S(1)}, u32[]{:S(2)}, u32[]{:S(2)}) async-start(bf16[32,2,8192]{2,1,0:T(2,128)(2,1)} %bitcast.6), calls=%async_computation.1 | async-start | bytes 2097152 | tf_op jit(solution)/shard_map/all_to_all | solution.py:51
  49.8 62.0 %all-to-all-start = ((bf16[32,2,8192]{2,1,0:T(2,128)(2,1)}), bf16[32,2,8192]{2,1,0:T(2,128)(2,1)S(1)}, u32[]{:S(2)}, u32[]{:S(2)}) async-start(bf16[32,2,8192]{2,1,0:T(2,128)(2,1)} %bitcast.1), calls=%async_computation | async-start | bytes 2097152 | tf_op jit(solution)/shard_map/all_to_all | solution.py:50
  55.8 56.0 %all-gather.2.cloned.1.call-start = ((), (), s32[]{:S(2)}) async-start(), calls=%async_computation.6 | async-start | bytes 1179648 | tf_op jit(solution)/shard_map/all_gather | solution.py:39
  117.4 9.5 copy-start.12
  117.4 193.5 %all-to-all-start.2 = ((bf16[32,2048,64]{1,2,0:T(8,128)(2,1)}), bf16[32,2048,64]{1,2,0:T(8,128)(2,1)}, u32[]{:S(2)}, u32[]{:S(2)}) async-start(bf16[32,2048,64]{1,2,0:T(8,128)(2,1)} %bitcast.189), calls=%async_computation.2 | async-start | bytes 16777216 | tf_op jit(solution)/shard_map/all_to_all | solution.py:41
  126.8 694.9 %reduce-scatter.2.cloned.1.call-start = ((), (), s32[]{:S(2)}) async-start(), calls=%async_computation.7 | async-start | bytes 18874368 | tf_op jit(solution)/shard_map/reduce_scatter | solution.py:152
  127.6 5.5 copy-start.3
  128.2 2.1 copy-start.5
  347.0 1.5 copy-start.1
  349.3 116.6 %copy-start.7 = (bf16[2,2048,128]{1,2,0:T(8,128)(2,1)S(1)}, bf16[2,2048,128]{1,2,0:T(8,128)(2,1)}, u32[]{:S(2)}) copy-start(bf16[2,2048,128]{1,2,0:T(8,128)(2,1)} %get-tuple-element.663) | copy-start | bytes 3145732 | tf_op jit(solution)/shard_map/while
  355.7 1.4 copy-start.10
  357.2 0.7 copy-start.11
  383.9 1.4 copy-start.10
  385.4 0.7 copy-start.11
  412.1 1.4 copy-start.10
  413.5 0.7 copy-start.11
  440.3 1.4 copy-start.10
  441.7 0.7 copy-start.11
  461.5 5.4 copy-start.2
  465.9 1.0 copy-start.8
  466.9 1.5 copy-start.1
  469.1 116.6 %copy-start.7 = (bf16[2,2048,128]{1,2,0:T(8,128)(2,1)S(1)}, bf16[2,2048,128]{1,2,0:T(8,128)(2,1)}, u32[]{:S(2)}) copy-start(bf16[2,2048,128]{1,2,0:T(8,128)(2,1)} %get-tuple-element.663) | copy-start | bytes 3145732 | tf_op jit(solution)/shard_map/while
  475.5 1.4 copy-start.10
  477.0 0.7 copy-start.11
  503.7 1.4 copy-start.10
  505.2 0.7 copy-start.11
  531.9 1.4 copy-start.10
  533.4 0.7 copy-start.11
  560.1 1.4 copy-start.10
  561.6 0.7 copy-start.11
  581.3 5.4 copy-start.2
  585.7 1.0 copy-start.8
  604.3 1.2 copy-start.9
  612.2 213.9 %all-to-all-start.3 = ((f32[2,32,8192]{2,0,1:T(2,128)}), f32[2,32,8192]{2,0,1:T(2,128)}, u32[]{:S(2)}, u32[]{:S(2)}) async-start(f32[2,32,8192]{2,0,1:T(2,128)} %copy.90), calls=%async_computation.3 | async-start | bytes 4194304 | tf_op jit(solution)/shard_map/all_to_all | solution.py:126
  622.6 215.1 %copy-start.6 = (bf16[1,2,32,8192]{3,2,1,0:T(8,128)(2,1)S(1)}, bf16[1,2,32,8192]{3,2,1,0:T(8,128)(2,1)}, u32[]{:S(2)}) copy-start(bf16[1,2,32,8192]{3,2,1,0:T(8,128)(2,1)} %copy-done.5) | copy-start | bytes 3145732
  826.1 12.9 %copy-start.4 = (bf16[1,2,32,8192]{3,2,1,0:T(8,128)(2,1)S(1)}, bf16[1,2,32,8192]{3,2,1,0:T(8,128)(2,1)}, u32[]{:S(2)}) copy-start(bf16[1,2,32,8192]{3,2,1,0:T(8,128)(2,1)} %copy-done.3) | copy-start | bytes 3145732
  826.2 61.6 %all-to-all-start.4 = ((f32[1,256,2048]{1,0,2:T(1,128)}), f32[1,256,2048]{1,0,2:T(1,128)}, u32[]{:S(2)}, u32[]{:S(2)}) async-start(f32[1,256,2048]{1,0,2:T(1,128)} %broadcast_in_dim.75), calls=%async_computation.5 | async-start | bytes 4194304 | tf_op jit(solution)/shard_map/all_to_all | solution.py:153
  837.7 259.5 %all-reduce.3.cloned.1.call-start = ((), (), s32[]{:S(2)}) async-start(), calls=%async_computation.8 | async-start | bytes 655360 | tf_op jit(solution)/shard_map/psum | solution.py:151
Sparse Core Ops, SparseCore 0:
  59.1 52.6 all-gather.1
  604.4 217.2 reduce-scatter.1
  845.3 251.8 all-reduce.2
where the time goes:
time: 1110 us
  waiting for transfers between devices  704 us (63%)
  local copies, waits for them, and re-layouts  209 us (19%)
  matrix products  97 us (9%)
  starting transfers between devices  48.5 us (4%)
  other arithmetic  20.5 us (2%)
  loops' own time  14.4 us (1%)
  between operations  14 us (1%)
    psum x1, waiting for transfers between devices, on_device(): lax.psum((proj_local / full_len, out_local / full_len), ('row', 'col'))  207 us
    reduce_scatter x1, waiting for transfers between devices, on_device(): lax.psum_scatter(bias_part, 'row', scatter_dimension=0, tiled=True)  199 us
    all_to_all x1, waiting for transfers between devices, on_device(): lax.all_to_all(copies, 'col', split_axis=0, concat_axis=2, tiled=True)[0]  178 us
    dynamic_update_slice x8, local copies, waits for them, and re-layouts, block_step(): acc = lax.dynamic_update_slice_in_dim(acc, previous + score_grad, start, 0)  93.7 us
    all_gather x1, waiting for transfers between devices, on_device(): bias_rows = lax.all_gather(bias_logits, 'row', axis=1, tiled=True)  55.3 us
    dot_general x8, matrix products, block_step(): jnp.dot(attn_grad, values_row.T, preferred_element_type=jnp.float32)  43.7 us
    all_to_all x1, waiting for transfers between devices, on_device(): lax.all_to_all(bias_share[None], 'col', split_axis=2, concat_axis=0, tile...  38.5 us
    all_to_all x1, waiting for transfers between devices, on_device(): lax.all_to_all(spread(grad_out), 'col', split_axis=0, concat_axis=2, tile...  25.4 us
  transfers between devices with their start and end apart: 8, of which 6 were waited for; matrix products, arithmetic and copies ran while one was open for 3% of the time, Pallas kernels for 0%

commit v1 on v0

v1 whole, which is shorter than its diff:
```python
import jax
import jax.numpy as jnp
import numpy as np
from jax import lax
from jax.experimental import pallas as pl
from jax.experimental.pallas import tpu as pltpu
from jax.sharding import Mesh
from jax.sharding import PartitionSpec as P

H = 4
D = 32
CHAINS = 4
NEG_BIG = -1e30
LOG2E = 1.4426950408889634
SCALE = D ** (-0.5)
F32 = jnp.float32
BF16 = jnp.bfloat16
QUAD = 4
TOK = 64
SUB = 16
COLS = 32
ROWS = 8
LEN = TOK * COLS
QRY = SUB * COLS
VMEM_LIMIT = 56 * 1024 * 1024


def dot(a, b, dims):
    return lax.dot_general(a, b, (dims, ((), ())), preferred_element_type=F32)


def nn(a, b):
    return dot(a, b, ((1,), (0,)))


def nt(a, b):
    return dot(a, b, ((1,), (1,)))


def tn(a, b):
    return dot(a, b, ((0,), (0,)))


def lane_group(shape):
    return (lax.broadcasted_iota(jnp.int32, shape, 1) // D) % QUAD


def swap_halves(x):
    return jnp.concatenate([x[:, TOK:], x[:, :TOK]], axis=1)


def bias_pack_kernel(limit_ref, perm_ref, bias_ref, out_ref):
    low = lax.broadcasted_iota(jnp.int32, (32, 128), 1) < 64
    valid = lax.broadcasted_iota(jnp.int32, (TOK, 256), 0) < limit_ref[0]
    for h in range(H):
        turned = tn(bias_ref[h], perm_ref[...])
        turned = jnp.where(valid, turned, NEG_BIG)
        for m in range(2):
            top = turned[:32, m * 128 : (m + 1) * 128]
            bottom = turned[32:, m * 128 : (m + 1) * 128]
            out_ref[h * 4 + 2 * m] = jnp.where(low, top, swap_halves(bottom)).astype(BF16)
            out_ref[h * 4 + 2 * m + 1] = jnp.where(low, swap_halves(top), bottom).astype(BF16)


def bias_unpack_kernel(perm_ref, parts_ref, out_ref):
    low = lax.broadcasted_iota(jnp.int32, (32, 128), 1) < 64
    for h in range(H):
        tops, bottoms = [], []
        for m in range(2):
            first = parts_ref[h * 4 + 2 * m].astype(F32)
            second = parts_ref[h * 4 + 2 * m + 1].astype(F32)
            tops.append(jnp.where(low, first, swap_halves(second)))
            bottoms.append(jnp.where(low, swap_halves(first), second))
        whole = jnp.concatenate(
            [jnp.concatenate(tops, axis=1), jnp.concatenate(bottoms, axis=1)], axis=0
        ).astype(BF16)
        out_ref[h] = nt(perm_ref[...], whole)


def project_kernel(pair_ref, grad_ref, wp_ref, wo_ref, send_ref, gates_ref, ograd_ref):
    wp = wp_ref[...]
    wo = wo_ref[...]
    group_p = lane_group(wp.shape)
    group_o = lane_group(wo.shape)
    zero = jnp.zeros((), BF16)
    wide_p = jnp.concatenate([jnp.where(group_p == r, wp, zero) for r in range(QUAD)], axis=0)
    wide_o = jnp.concatenate([jnp.where(group_o == r, wo, zero) for r in range(QUAD)], axis=0)

    def quads(ref):
        return jnp.concatenate(
            [
                jnp.concatenate([ref[4 * q + r] for r in range(QUAD)], axis=1)
                for q in range(4)
            ],
            axis=0,
        )

    proj = nn(quads(pair_ref), wide_p).astype(BF16)
    ograd = nn(quads(grad_ref), wide_o).astype(BF16)
    for q in range(4):
        rows = slice(q * TOK, (q + 1) * TOK)
        qq = q % 2
        for h in range(H):
            query, key, value, gate = [
                proj[rows, h * 512 + p * 128 : h * 512 + (p + 1) * 128] for p in range(4)
            ]
            og = ograd[rows, h * 128 : (h + 1) * 128]
            gates_ref[q, :, h * 128 : (h + 1) * 128] = gate
            ograd_ref[q, :, h * 128 : (h + 1) * 128] = og
            cot = (og.astype(F32) * jax.nn.sigmoid(gate.astype(F32))).astype(BF16)
            for j in range(4):
                dest = (q // 2) * 16 + h * 4 + j
                send_ref[dest, qq * TOK : (qq + 1) * TOK] = value if j % 2 else key
                part = slice(j * SUB, (j + 1) * SUB)
                send_ref[dest, 128 + qq * SUB : 128 + (qq + 1) * SUB] = query[part]
                send_ref[dest, 160 + qq * SUB : 160 + (qq + 1) * SUB] = cot[part]


CHUNK = 256


def attend_kernel(
    core_ref,
    recv_ref,
    other_ref,
    bias_ref,
    kv_out,
    qo_out,
    bg_out,
    b32,
    s_ref,
    acc,
    kq,
    vq,
    kqt,
    vqt,
    dk,
    dv,
):
    core = core_ref[0]
    low = lax.broadcasted_iota(jnp.int32, (32, 128), 1) < 64

    def build(n, _):
        yl, blk = n // 16, n % 16
        at = pl.multiple_of(n * 64, 64)
        for m in range(4):
            left = bias_ref[4 * m + yl, blk].astype(F32) * LOG2E
            right = bias_ref[4 * m + 2 + yl, blk].astype(F32) * LOG2E
            lanes = slice(m * 128, (m + 1) * 128)
            b32[pl.ds(at, 32), lanes] = jnp.where(low, left, swap_halves(right))
            b32[pl.ds(at + 32, 32), lanes] = jnp.where(low, swap_halves(left), right)
        return 0

    lax.fori_loop(0, 32, build, 0)
    acc[...] = jnp.zeros_like(acc)
    steps = LEN // CHUNK

    def quad(q, _):
        at = pl.multiple_of(q * TOK, TOK)
        mine = recv_ref[:, pl.ds(at, TOK), :].reshape(LEN, 128)
        theirs = other_ref[:, pl.ds(at, TOK), :].reshape(LEN, 128)
        keys = jnp.where(core == 0, mine, theirs)
        values = jnp.where(core == 0, theirs, mine)
        kq[...] = keys
        vq[...] = values
        kqt[...] = keys.T
        vqt[...] = values.T
        sub = pl.multiple_of(q * SUB, SUB)
        query = recv_ref[:, pl.ds(128 + sub, SUB), :].reshape(QRY, 128)
        cot = recv_ref[:, pl.ds(160 + sub, SUB), :].reshape(QRY, 128)
        query_t = query.T
        cot_t = cot.T
        dk[...] = jnp.zeros_like(dk)
        dv[...] = jnp.zeros_like(dv)
        lanes = lane_group((QRY, 128))
        subs = lax.broadcasted_iota(jnp.int32, (128, QRY), 0) // D
        zero = jnp.zeros((), BF16)
        out_t, dq_t = [], []
        for i in range(QUAD):
            band = slice(i * D, (i + 1) * D)
            q_m = jnp.where(lanes == i, query, zero)
            c_m = jnp.where(lanes == i, cot, zero)
            qt_m = jnp.where(subs == i, query_t, zero)
            ct_m = jnp.where(subs == i, cot_t, zero)

            def score(c, top, qt_m=qt_m):
                rows = pl.ds(pl.multiple_of(c * CHUNK, CHUNK), CHUNK)
                s = nn(kq[rows, :], qt_m) * (SCALE * LOG2E) + b32[rows, :]
                s_ref[rows, :] = s
                return jnp.maximum(top, jnp.max(s.reshape(CHUNK // 8, 8, QRY), axis=0))

            top = lax.fori_loop(0, steps, score, jnp.full((8, QRY), -3e38, F32), unroll=2)
            top = jnp.max(top, axis=0, keepdims=True)

            def weigh(c, carry, band=band, top=top):
                total, out = carry
                rows = pl.ds(pl.multiple_of(c * CHUNK, CHUNK), CHUNK)
                e = jnp.exp2(s_ref[rows, :] - top)
                s_ref[rows, :] = e
                total = total + jnp.sum(e.reshape(CHUNK // 8, 8, QRY), axis=0)
                out = out + nn(vqt[band, rows], e.astype(BF16))
                return total, out

            total, out = lax.fori_loop(
                0,
                steps,
                weigh,
                (jnp.zeros((8, QRY), F32), jnp.zeros((D, QRY), F32)),
                unroll=2,
            )
            inv = 1.0 / jnp.sum(total, axis=0, keepdims=True)
            out = out * inv
            delta = jnp.sum(cot_t[band].astype(F32) * out, axis=0, keepdims=True)

            def back(c, dq, band=band, inv=inv, delta=delta, q_m=q_m, c_m=c_m, ct_m=ct_m):
                rows = pl.ds(pl.multiple_of(c * CHUNK, CHUNK), CHUNK)
                prob = s_ref[rows, :] * inv
                ds = prob * (nn(vq[rows, :], ct_m) - delta)
                acc[rows, :] += ds
                half = ds.astype(BF16)
                dk[rows, :] += nn(half, q_m)
                dv[rows, :] += nn(prob.astype(BF16), c_m)
                return dq + nn(kqt[band, rows], half)

            dq = lax.fori_loop(0, steps, back, jnp.zeros((D, QRY), F32), unroll=2)
            out_t.append(out)
            dq_t.append(dq * SCALE)
        qo_out[:, pl.ds(sub, SUB), :] = (
            jnp.concatenate(dq_t, axis=0).T.astype(BF16).reshape(COLS, SUB, 128)
        )
        qo_out[:, pl.ds(32 + sub, SUB), :] = (
            jnp.concatenate(out_t, axis=0).T.astype(BF16).reshape(COLS, SUB, 128)
        )
        kv_out[core, :, pl.ds(at, TOK), :] = (
            (dk[...] * SCALE).astype(BF16).reshape(COLS, TOK, 128)
        )
        kv_out[1 - core, :, pl.ds(at, TOK), :] = dv[...].astype(BF16).reshape(COLS, TOK, 128)
        return 0

    lax.fori_loop(0, 2, quad, 0)

    def spread(n, _):
        yl, blk = n // 16, n % 16
        at = pl.multiple_of(n * 64, 64)
        for m in range(4):
            lanes = slice(m * 128, (m + 1) * 128)
            top = acc[pl.ds(at, 32), lanes]
            bottom = acc[pl.ds(at + 32, 32), lanes]
            bg_out[4 * m + yl, blk] = jnp.where(low, top, swap_halves(bottom)).astype(BF16)
            bg_out[4 * m + 2 + yl, blk] = jnp.where(low, swap_halves(top), bottom).astype(BF16)
        return 0

    lax.fori_loop(0, 32, spread, 0)


def finish_kernel(
    recv_ref, gates_ref, ograd_ref, pair_ref, grad_ref, wp_ref, pair_out, weight_out, pg, gt
):
    for q in range(4):
        rows = slice(q * TOK, (q + 1) * TOK)
        qq = q % 2
        wide = slice(qq * TOK, (qq + 1) * TOK)
        for h in range(H):
            base = (q // 2) * 16 + h * 4
            key = recv_ref[base, wide].astype(F32) + recv_ref[base + 2, wide].astype(F32)
            value = recv_ref[base + 1, wide].astype(F32) + recv_ref[base + 3, wide].astype(F32)
            query = jnp.concatenate(
                [recv_ref[base + j, 128 + qq * SUB : 128 + (qq + 1) * SUB] for j in range(4)],
                axis=0,
            )
            out = jnp.concatenate(
                [recv_ref[base + j, 160 + qq * SUB : 160 + (qq + 1) * SUB] for j in range(4)],
                axis=0,
            ).astype(F32)
            lanes = slice(h * 128, (h + 1) * 128)
            sig = jax.nn.sigmoid(gates_ref[q, :, lanes].astype(F32))
            og = ograd_ref[q, :, lanes].astype(F32)
            gt[rows, lanes] = (sig * out).astype(BF16)
            pg[rows, h * 512 : h * 512 + 128] = query
            pg[rows, h * 512 + 128 : h * 512 + 256] = key.astype(BF16)
            pg[rows, h * 512 + 256 : h * 512 + 384] = value.astype(BF16)
            pg[rows, h * 512 + 384 : h * 512 + 512] = (og * out * sig * (1.0 - sig)).astype(BF16)
    wp = wp_ref[...]
    group = lane_group(wp.shape)
    zero = jnp.zeros((), BF16)
    grads = pg[...]
    gated = gt[...]
    for r in range(QUAD):
        part = nt(grads, jnp.where(group == r, wp, zero)).astype(BF16)
        for q in range(4):
            pair_out[4 * q + r] = part[q * TOK : (q + 1) * TOK]
    turned = grads.T
    gated_t = gated.T
    for r in range(QUAD):
        pair_r = jnp.concatenate([pair_ref[4 * q + r] for q in range(4)], axis=0)
        grad_r = jnp.concatenate([grad_ref[4 * q + r] for q in range(4)], axis=0)
        for n in range(16):
            at = n * 128 + r * D
            piece = nn(turned[at : at + D], pair_r) * (1.0 / LEN)
            if r == 0:
                weight_out[n * D : (n + 1) * D] = piece
            else:
                weight_out[n * D : (n + 1) * D] += piece
        for n in range(4):
            at = n * 128 + r * D
            piece = nn(gated_t[at : at + D], grad_r) * (1.0 / LEN)
            where = slice(512 + n * D, 512 + (n + 1) * D)
            if r == 0:
                weight_out[where] = piece
            else:
                weight_out[where] += piece


def whole():
    return pl.BlockSpec(memory_space=pltpu.VMEM)


def scalar():
    return pl.BlockSpec(memory_space=pltpu.SMEM)


def call(kernel, in_specs, outs, scratch=(), flops=0, moved=0):
    return pl.pallas_call(
        kernel,
        out_shape=outs,
        in_specs=in_specs,
        out_specs=jax.tree.map(lambda _: whole(), outs),
        scratch_shapes=list(scratch),
        compiler_params=pltpu.CompilerParams(vmem_limit_bytes=VMEM_LIMIT),
        cost_estimate=pl.CostEstimate(flops=flops, bytes_accessed=moved, transcendentals=0),
    )


def shape(dims, dtype=BF16):
    return jax.ShapeDtypeStruct(dims, dtype)


def query_order():
    perm = np.zeros((256, 256), np.float32)
    for s in range(4):
        for j in range(4):
            for t in range(SUB):
                perm[s * 64 + j * SUB + t, j * 64 + s * SUB + t] = 1.0
    return perm


def widen(groups):
    source = lax.broadcasted_iota(jnp.int32, (groups * D, groups * 128), 0)
    target = lax.broadcasted_iota(jnp.int32, (groups * D, groups * 128), 1)
    same = (source // D == target // 128) & (source % D == target % D)
    return same.astype(BF16)


def on_device(pair_rep, w_proj, bias_logits, chain_lengths, w_out, grad_out):
    block = lax.axis_index(("yl", "z", "c"))
    core = lax.axis_index("c")
    col = ("yl", "z", "c")
    plane = ("yh", "x", "yl")
    per_chain = COLS // CHAINS
    chain = lax.dynamic_index_in_dim(chain_lengths, block // per_chain, 0, keepdims=True)
    limit = chain - (block % per_chain) * TOK
    perm = jnp.asarray(query_order(), BF16)

    packed = call(bias_pack_kernel, [scalar(), whole(), whole()], shape((16, 32, 128)))(
        limit, perm, bias_logits
    )
    bias_z = lax.all_to_all(packed, ("z", "c"), 0, 0, tiled=True)
    bias_all = lax.all_to_all(
        jnp.broadcast_to(bias_z[None], (16, 16, 32, 128)), plane, 0, 0, tiled=True
    )

    wp = jnp.dot(w_proj, widen(16), preferred_element_type=F32).astype(BF16)
    wo = jnp.dot(w_out.T, widen(4), preferred_element_type=F32).astype(BF16)
    send, gates, ograd = call(
        project_kernel,
        [whole()] * 4,
        (shape((COLS, 192, 128)), shape((4, TOK, 512)), shape((4, TOK, 512))),
        flops=700_000_000,
        moved=6_000_000,
    )(pair_rep, grad_out, wp, wo)
    recv = lax.all_to_all(send, col, 0, 0, tiled=True)
    other = lax.ppermute(recv[:, :128], "c", [(0, 1), (1, 0)])
    kv, qo, bg = call(
        attend_kernel,
        [scalar(), whole(), whole(), whole()],
        (shape((2, COLS, 128, 128)), shape((COLS, 64, 128)), shape((16, 16, 32, 128))),
        [
            pltpu.VMEM((LEN, QRY), F32),
            pltpu.VMEM((LEN, QRY), F32),
            pltpu.VMEM((LEN, QRY), F32),
            pltpu.VMEM((LEN, 128), BF16),
            pltpu.VMEM((LEN, 128), BF16),
            pltpu.VMEM((128, LEN), BF16),
            pltpu.VMEM((128, LEN), BF16),
            pltpu.VMEM((LEN, 128), F32),
            pltpu.VMEM((LEN, 128), F32),
        ],
        flops=30_000_000_000,
        moved=10_000_000,
    )(core[None].astype(jnp.int32), recv, other, bias_all)
    given = lax.ppermute(kv[1], "c", [(0, 1), (1, 0)])
    kept = (kv[0].astype(F32) + given.astype(F32)).astype(BF16)
    home = lax.all_to_all(jnp.concatenate([kept, qo], axis=1), col, 0, 0, tiled=True)
    bg_parts = lax.all_to_all(bg, plane, 0, 0, tiled=True)
    bg_sum = jnp.sum(bg_parts.astype(F32), axis=0).astype(BF16)
    bg_home = lax.all_to_all(bg_sum, ("z", "c"), 0, 0, tiled=True)
    bias_grad = call(bias_unpack_kernel, [whole()] * 2, shape((H, 256, TOK), F32))(perm, bg_home)
    pair_grad, weights = call(
        finish_kernel,
        [whole()] * 6,
        (shape((16, TOK, 128)), shape((640, 128), F32)),
        [pltpu.VMEM((256, 2048), BF16), pltpu.VMEM((256, 512), BF16)],
        flops=1_000_000_000,
        moved=4_000_000,
    )(home, gates, ograd, pair_rep, grad_out, wp)
    every = ("yh", "x", "yl", "z", "c")
    pieces = jnp.pad(weights, ((0, 128), (0, 0))).reshape(256, 3, 128)
    summed = jnp.sum(lax.all_to_all(pieces, every, 0, 0, tiled=True), axis=0)
    total = lax.all_to_all(
        jnp.broadcast_to(summed[None], (256, 3, 128)), every, 0, 0, tiled=True
    ).reshape(768, 128)
    return (pair_grad, bias_grad, total[:512].T, total[512:640])


def solution(mesh):
    fine = Mesh(mesh.devices.reshape(2, 4, 2, 8, 2), ("yh", "x", "yl", "z", "c"))
    row = ("yh", "x")
    col = ("yl", "z", "c")
    return jax.shard_map(
        on_device,
        mesh=fine,
        in_specs=(
            P(row, col, None),
            P(),
            P(None, row, col),
            P(),
            P(),
            P(row, col, None),
        ),
        out_specs=(P(row, col, None), P(None, row, col), P(), P()),
        check_vma=False,
    )
```

time: 1110 us -> 320 us (0.29)
  waiting for transfers between devices: 704 us -> 91.6 us
  local copies, waits for them, and re-layouts: 209 us -> 14 us
  matrix products: 97 us -> 3.06 us
  blocking collectives: 0 us -> 89 us
  Pallas kernels: 0 us -> 68.2 us
  other arithmetic: 20.5 us -> 1.8 us
  loops' own time: 14.4 us -> 0 us
  between operations: 14 us -> 1.52 us
    psum x1 -> x0, waiting for transfers between devices: 207 us -> none  [on_device(): lax.psum((proj_local / full_len, out_local / full_len), ('row', 'col'))]
    reduce_scatter x1 -> x0, waiting for transfers between devices: 199 us -> none  [on_device(): lax.psum_scatter(bias_part, 'row', scatter_dimension=0, tiled=True)]
    all_to_all x5 -> x6, waiting for transfers between devices: 242 us -> 89.3 us  [the longest x1 23.3 us: on_device(): lax.all_to_all(jnp.broadcast_to(bias_z[None], (16, 16, 32, 128)), plane,...]
    dynamic_update_slice x11 -> x0, local copies, waits for them, and re-layouts: 95.4 us -> none  [the longest x8 93.7 us: block_step(): acc = lax.dynamic_update_slice_in_dim(acc, previous + score_grad, start, 0)]
    dot_general x53 -> x2, matrix products: 97 us -> 3.06 us  [the longest x1 2.06 us: on_device(): wp = jnp.dot(w_proj, widen(16), preferred_element_type=F32).astype(BF16)]
    all_to_all x0 -> x2, blocking collectives: none -> 89 us  [the longest x1 44.7 us: on_device(): recv = lax.all_to_all(send, col, 0, 0, tiled=True)]
    pallas_call x0 -> x5, Pallas kernels: none -> 68.2 us  [the longest x1 56.1 us: on_device(): call(attend_kernel, [scalar(), whole(), whole(), whole()], (shape((2, COL...]
    all_gather x1 -> x0, waiting for transfers between devices: 55.3 us -> none  [on_device(): bias_rows = lax.all_gather(bias_logits, 'row', axis=1, tiled=True)]
  transfers between devices with their start and end apart: 8 -> 8, of which waited for: 6 -> 7; matrix products, arithmetic and copies ran while one was open for 3% -> 3% of each run, Pallas kernels for 0% -> 3%
where the time goes in v1:
time: 320 us; the launch traced here: 319 us
  waiting for transfers between devices  91.6 us (29%)
  blocking collectives  89 us (28%)
  Pallas kernels  68.2 us (21%)
  starting transfers between devices  50.2 us (16%)
  local copies, waits for them, and re-layouts  14 us (4%)
    pallas_call x1, Pallas kernels, on_device(): call(attend_kernel, [scalar(), whole(), whole(), whole()], (shape((2, COL...  56.1 us
    all_to_all x1, blocking collectives, on_device(): recv = lax.all_to_all(send, col, 0, 0, tiled=True)  44.7 us
    all_to_all x1, blocking collectives, on_device(): lax.all_to_all(jnp.concatenate([kept, qo], axis=1), col, 0, 0, tiled=True)  44.3 us
    all_to_all x1, waiting for transfers between devices, on_device(): lax.all_to_all(jnp.broadcast_to(bias_z[None], (16, 16, 32, 128)), plane,...  23.3 us
    all_to_all x1, waiting for transfers between devices, on_device(): bg_parts = lax.all_to_all(bg, plane, 0, 0, tiled=True)  19.4 us
    all_to_all x1, waiting for transfers between devices, on_device(): summed = jnp.sum(lax.all_to_all(pieces, every, 0, 0, tiled=True), axis=0)  19.1 us
    all_to_all x1, waiting for transfers between devices, on_device(): lax.all_to_all(jnp.broadcast_to(summed[None], (256, 3, 128)), every, 0, 0...  15.9 us
    all_to_all x1, starting transfers between devices, on_device(): summed = jnp.sum(lax.all_to_all(pieces, every, 0, 0, tiled=True), axis=0)  12.4 us
  transfers between devices with their start and end apart: 8, of which 7 were waited for; matrix products, arithmetic and copies ran while one was open for 3% of the time, Pallas kernels for 3%

profile of v1, /device:TPU:1, one launch (start us, length us, event | category | flops | bytes accessed | tf_op | source)
XLA Modules:
  0.0 319.3 jit_solution(11039819936514769729)
XLA Ops:
  0.6 0.0 copy-start
  0.7 1.8 copy.18.bias_ref
  2.5 1.2 dynamic_slice.4
  4.3 2.0 shard_map.103
  6.4 10.0 %all-to-all-start.1 = ((bf16[16,32,128]{2,1,0:T(8,128)(2,1)}), bf16[16,32,128]{2,1,0:T(8,128)(2,1)S(1)}, u32[]{:S(2)}, u32[]{:S(2)}) async-start(bf16[16,32,128]{2,1,0:T(8,128)(2,1)} %shard_map.103), calls=%async_computation.1 | async-start | bytes 262144 | tf_op jit(solution)/shard_map/all_to_all | solution.py:367
  16.5 0.0 copy-done
  16.5 0.0 copy-start.6
  16.5 2.1 fusion.6.wp_ref
  18.5 0.0 copy-done.6
  18.5 1.0 fusion.22.wo_ref
  19.5 3.4 %shard_map.102 = (bf16[32,192,128]{2,1,0:T(8,128)(2,1)}, bf16[4,64,512]{2,1,0:T(8,128)(2,1)}, bf16[4,64,512]{2,1,0:T(8,128)(2,1)}) custom-call(bf16[16,64,128]{2,1,0:T(8,128)(2,1)} %pair_ref.3, bf16[16,64,128]{2,1,0:T(8,128)(2,1)} %grad_ref.3, bf16[128,2048]{1,0:T(8,128)(2,1)} %fusion.6.wp_ref, bf16[128,512]{1,0:T(8,128)(2,1)} %fusion.22.wo_ref), custom_call_target="tpu_custom_call" | custom-call | flops 700000000 | bytes 6000000 | tf_op jit(solution)/shard_map/pallas_call | solution.py:374
  22.9 2.6 all-to-all-done.1
  25.5 44.7 %all_to_all.40.recv_ref = bf16[32,192,128]{2,1,0:T(8,128)(2,1)S(1)} all-to-all(bf16[32,192,128]{2,1,0:T(8,128)(2,1)} %get-tuple-element.12), channel_id=1, replica_groups=mesh['yh'=2,'x'=4,'yl'=2,'z'=8,'c'=2] {'yl','z','c'}, dimensions={0} | all-to-all | bytes 3145728 | tf_op jit(solution)/shard_map/all_to_all | solution.py:381
  70.2 0.0 copy-start.1
  70.2 1.9 broadcast_in_dim.7
  72.1 6.5 %all-to-all-start.2 = ((bf16[16,16,32,128]{3,2,1,0:T(8,128)(2,1)}), bf16[16,16,32,128]{3,2,1,0:T(8,128)(2,1)}, u32[]{:S(2)}, u32[]{:S(2)}) async-start(bf16[16,16,32,128]{3,2,1,0:T(8,128)(2,1)} %broadcast_in_dim.7), calls=%async_computation.2 | async-start | bytes 4194304 | tf_op jit(solution)/shard_map/all_to_all | solution.py:368
  78.6 0.0 copy-done.1
  78.6 0.1 slice.20
  78.7 2.7 collective-permute-start
  81.4 23.3 %all-to-all-done.2.bias_ref = bf16[16,16,32,128]{3,2,1,0:T(8,128)(2,1)} async-done(((bf16[16,16,32,128]{3,2,1,0:T(8,128)(2,1)}), bf16[16,16,32,128]{3,2,1,0:T(8,128)(2,1)}, u32[]{:S(2)}, u32[]{:S(2)}) %all-to-all-start.2) | async-done | bytes 2097184 | tf_op jit(solution)/shard_map/all_to_all | solution.py:368
  104.7 0.0 collective-permute-done.other_ref
  104.7 0.0 copy-start.5
  104.7 1.1 copy-done.5
  105.7 56.1 %shard_map.104 = (bf16[2,32,128,128]{3,2,1,0:T(8,128)(2,1)}, bf16[32,64,128]{2,1,0:T(8,128)(2,1)}, bf16[16,16,32,128]{3,2,1,0:T(8,128)(2,1)}) custom-call(s32[1]{0:T(128)} %bitcast.core_ref, bf16[32,192,128]{2,1,0:T(8,128)(2,1)} %copy-done.1, bf16[32,128,128]{2,1,0:T(8,128)(2,1)} %copy-done.5, bf16[16,16,32,128]{3,2,1,0:T(8,128)(2,1)} %all-to-all-done.2.bias_ref), custom_call_target="tpu_custom_call" | custom-call | flops 30000001024 | bytes 10000000 | tf_op jit(solution)/shard_map/pallas_call | solution.py:383
  161.8 0.0 copy-start.2
  161.8 1.4 slice_bitcast_fusion
  163.3 0.0 copy-start.4
  163.3 5.3 %collective-permute-start.1 = (bf16[32,128,128]{2,1,0:T(8,128)(2,1)S(1)}, bf16[32,128,128]{2,1,0:T(8,128)(2,1)S(1)}, u32[]{:S(2)}, u32[]{:S(2)}) collective-permute-start(bf16[32,128,128]{2,1,0:T(8,128)(2,1)S(1)} %slice_bitcast_fusion), channel_id=1, source_target_pairs={{0,1},{1,0},{2,3},{3,2},{4,5},{5,4},{6,7},{7,6},{8,9},{9,8},{10,11... | collective-permute-start | bytes 3145736 | tf_op jit(solution)/shard_map/ppermute | solution.py:401
  168.6 2.3 collective-permute-done.1
  170.9 0.0 copy-done.2
  170.9 0.4 fusion.9
  171.3 0.0 copy-done.4
  171.3 0.1 pad_maximum_fusion
  171.4 44.3 %all_to_all.41.recv_ref = bf16[32,192,128]{2,1,0:T(8,128)(2,1)} all-to-all(bf16[32,192,128]{2,1,0:T(8,128)(2,1)S(1)} %pad_maximum_fusion), channel_id=1, replica_groups=mesh['yh'=2,'x'=4,'yl'=2,'z'=8,'c'=2] {'yl','z','c'}, dimensions={0} | all-to-all | bytes 3145728 | tf_op jit(solution)/shard_map/all_to_all | solution.py:403
  215.7 3.9 %all-to-all-start.4 = ((bf16[16,16,32,128]{3,2,1,0:T(8,128)(2,1)}), bf16[16,16,32,128]{3,2,1,0:T(8,128)(2,1)S(1)}, u32[]{:S(2)}, u32[]{:S(2)}) async-start(bf16[16,16,32,128]{3,2,1,0:T(8,128)(2,1)} %get-tuple-element.18), calls=%async_computation.4 | async-start | bytes 4194304 | tf_op jit(solution)/shard_map/all_to_all | solution.py:404
  219.6 4.6 %shard_map.105 = (bf16[16,64,128]{2,1,0:T(8,128)(2,1)}, f32[640,128]{1,0:T(8,128)}) custom-call(bf16[32,192,128]{2,1,0:T(8,128)(2,1)} %all_to_all.41.recv_ref, bf16[4,64,512]{2,1,0:T(8,128)(2,1)} %get-tuple-element.15.gates_ref, bf16[4,64,512]{2,1,0:T(8,128)(2,1)} %get-tuple-element.16.ograd_ref, bf16[16,64,128]{2,1,0:T(8,128)(2,1)} %pair_ref.3, ...), custom_call_target="tpu_custom_call" | custom-call | flops 1000000000 | bytes 4000000 | tf_op jit(solution)/shard_map/pallas_call | solution.py:408
  224.2 1.0 pad.4
  225.2 1.0 reshape.18
  226.2 19.4 %all-to-all-done.4 = bf16[16,16,32,128]{3,2,1,0:T(8,128)(2,1)S(1)} async-done(((bf16[16,16,32,128]{3,2,1,0:T(8,128)(2,1)}), bf16[16,16,32,128]{3,2,1,0:T(8,128)(2,1)S(1)}, u32[]{:S(2)}, u32[]{:S(2)}) %all-to-all-start.4) | async-done | bytes 2097184 | tf_op jit(solution)/shard_map/all_to_all | solution.py:404
  245.5 12.4 %all-to-all-start.6 = ((f32[256,3,128]{2,1,0:T(4,128)}), f32[256,3,128]{2,1,0:T(4,128)S(1)}, u32[]{:S(2)}, u32[]{:S(2)}) async-start(f32[256,3,128]{2,1,0:T(4,128)} %reshape.18), calls=%async_computation.6 | async-start | bytes 1048576 | tf_op jit(solution)/shard_map/all_to_all | solution.py:418
  258.0 1.0 reduce_sum.21
  259.0 19.1 %all-to-all-done.6 = f32[256,3,128]{2,1,0:T(4,128)S(1)} async-done(((f32[256,3,128]{2,1,0:T(4,128)}), f32[256,3,128]{2,1,0:T(4,128)S(1)}, u32[]{:S(2)}, u32[]{:S(2)}) %all-to-all-start.6) | async-done | bytes 393248 | tf_op jit(solution)/shard_map/all_to_all | solution.py:418
  278.1 4.3 %all-to-all-start.5 = ((bf16[16,32,128]{2,1,0:T(8,128)(2,1)}), bf16[16,32,128]{2,1,0:T(8,128)(2,1)S(1)}, u32[]{:S(2)}, u32[]{:S(2)}) async-start(bf16[16,32,128]{2,1,0:T(8,128)(2,1)} %reduce_sum.21), calls=%async_computation.5 | async-start | bytes 262144 | tf_op jit(solution)/shard_map/all_to_all | solution.py:406
  282.4 0.3 reduce_sum.22
  282.7 8.9 %all-to-all-done.5.parts_ref = bf16[16,32,128]{2,1,0:T(8,128)(2,1)S(1)} async-done(((bf16[16,32,128]{2,1,0:T(8,128)(2,1)}), bf16[16,32,128]{2,1,0:T(8,128)(2,1)S(1)}, u32[]{:S(2)}, u32[]{:S(2)}) %all-to-all-start.5) | async-done | bytes 131104 | tf_op jit(solution)/shard_map/all_to_all | solution.py:406
  291.6 0.0 copy-start.3
  291.6 0.9 broadcast_in_dim.8
  292.5 5.2 %all-to-all-start.7 = ((f32[256,3,128]{2,1,0:T(4,128)}), f32[256,3,128]{2,1,0:T(4,128)S(1)}, u32[]{:S(2)}, u32[]{:S(2)}) async-start(f32[256,3,128]{2,1,0:T(4,128)} %broadcast_in_dim.8), calls=%async_computation.7 | async-start | bytes 1048576 | tf_op jit(solution)/shard_map/all_to_all | solution.py:419
  297.6 0.0 copy-done.3
  297.7 2.1 shard_map.106
  299.8 1.9 copy.19
  301.7 15.9 %all-to-all-done.7 = f32[256,3,128]{2,1,0:T(4,128)S(1)} async-done(((f32[256,3,128]{2,1,0:T(4,128)}), f32[256,3,128]{2,1,0:T(4,128)S(1)}, u32[]{:S(2)}, u32[]{:S(2)}) %all-to-all-start.7) | async-done | bytes 393248 | tf_op jit(solution)/shard_map/all_to_all | solution.py:419
  317.7 0.2 reshape.19
  317.8 0.6 slice.22
  318.5 0.8 copy.20
  (12 shorter events, 0.1 us)
Async XLA Ops:
  0.6 15.8 %copy-start = (bf16[128,512]{1,0:T(8,128)(2,1)S(1)}, bf16[128,512]{1,0:T(8,128)(2,1)}, u32[]{:S(2)}) copy-start(bf16[128,512]{1,0:T(8,128)(2,1)} %param.8) | copy-start | bytes 393220
  6.4 19.1 %all-to-all-start.1 = ((bf16[16,32,128]{2,1,0:T(8,128)(2,1)}), bf16[16,32,128]{2,1,0:T(8,128)(2,1)S(1)}, u32[]{:S(2)}, u32[]{:S(2)}) async-start(bf16[16,32,128]{2,1,0:T(8,128)(2,1)} %shard_map.103), calls=%async_computation.1 | async-start | bytes 262144 | tf_op jit(solution)/shard_map/all_to_all | solution.py:367
  16.5 2.1 copy-start.6
  70.2 8.4 %copy-start.1 = (bf16[32,192,128]{2,1,0:T(8,128)(2,1)}, bf16[32,192,128]{2,1,0:T(8,128)(2,1)S(1)}, u32[]{:S(2)}) copy-start(bf16[32,192,128]{2,1,0:T(8,128)(2,1)S(1)} %all_to_all.40.recv_ref) | copy-start | bytes 4718596
  72.1 32.6 %all-to-all-start.2 = ((bf16[16,16,32,128]{3,2,1,0:T(8,128)(2,1)}), bf16[16,16,32,128]{3,2,1,0:T(8,128)(2,1)}, u32[]{:S(2)}, u32[]{:S(2)}) async-start(bf16[16,16,32,128]{3,2,1,0:T(8,128)(2,1)} %broadcast_in_dim.7), calls=%async_computation.2 | async-start | bytes 4194304 | tf_op jit(solution)/shard_map/all_to_all | solution.py:368
  78.7 26.0 %collective-permute-start = (bf16[32,128,128]{2,1,0:T(8,128)(2,1)S(1)}, bf16[32,128,128]{2,1,0:T(8,128)(2,1)S(1)}, u32[]{:S(2)}, u32[]{:S(2)}) collective-permute-start(bf16[32,128,128]{2,1,0:T(8,128)(2,1)S(1)} %slice.20), channel_id=1, source_target_pairs={{0,1},{1,0},{2,3},{3,2},{4,5},{5,4},{6,7},{7,6},{8,9},{9,8},{10,11... | collective-permute-start | bytes 3145736 | tf_op jit(solution)/shard_map/ppermute | solution.py:382
  104.7 1.1 copy-start.5
  161.8 9.1 %copy-start.2 = (bf16[2,32,128,128]{3,2,1,0:T(8,128)(2,1)S(1)}, bf16[2,32,128,128]{3,2,1,0:T(8,128)(2,1)}, u32[]{:S(2)}) copy-start(bf16[2,32,128,128]{3,2,1,0:T(8,128)(2,1)} %get-tuple-element.13) | copy-start | bytes 6291460
  163.3 8.0 %copy-start.4 = (bf16[32,64,128]{2,1,0:T(8,128)(2,1)S(1)}, bf16[32,64,128]{2,1,0:T(8,128)(2,1)}, u32[]{:S(2)}) copy-start(bf16[32,64,128]{2,1,0:T(8,128)(2,1)} %get-tuple-element.14) | copy-start | bytes 1572868
  163.3 7.6 %collective-permute-start.1 = (bf16[32,128,128]{2,1,0:T(8,128)(2,1)S(1)}, bf16[32,128,128]{2,1,0:T(8,128)(2,1)S(1)}, u32[]{:S(2)}, u32[]{:S(2)}) collective-permute-start(bf16[32,128,128]{2,1,0:T(8,128)(2,1)S(1)} %slice_bitcast_fusion), channel_id=1, source_target_pairs={{0,1},{1,0},{2,3},{3,2},{4,5},{5,4},{6,7},{7,6},{8,9},{9,8},{10,11... | collective-permute-start | bytes 3145736 | tf_op jit(solution)/shard_map/ppermute | solution.py:401
  215.7 29.9 %all-to-all-start.4 = ((bf16[16,16,32,128]{3,2,1,0:T(8,128)(2,1)}), bf16[16,16,32,128]{3,2,1,0:T(8,128)(2,1)S(1)}, u32[]{:S(2)}, u32[]{:S(2)}) async-start(bf16[16,16,32,128]{3,2,1,0:T(8,128)(2,1)} %get-tuple-element.18), calls=%async_computation.4 | async-start | bytes 4194304 | tf_op jit(solution)/shard_map/all_to_all | solution.py:404
  245.5 32.5 %all-to-all-start.6 = ((f32[256,3,128]{2,1,0:T(4,128)}), f32[256,3,128]{2,1,0:T(4,128)S(1)}, u32[]{:S(2)}, u32[]{:S(2)}) async-start(f32[256,3,128]{2,1,0:T(4,128)} %reshape.18), calls=%async_computation.6 | async-start | bytes 1048576 | tf_op jit(solution)/shard_map/all_to_all | solution.py:418
  278.1 13.5 %all-to-all-start.5 = ((bf16[16,32,128]{2,1,0:T(8,128)(2,1)}), bf16[16,32,128]{2,1,0:T(8,128)(2,1)S(1)}, u32[]{:S(2)}, u32[]{:S(2)}) async-start(bf16[16,32,128]{2,1,0:T(8,128)(2,1)} %reduce_sum.21), calls=%async_computation.5 | async-start | bytes 262144 | tf_op jit(solution)/shard_map/all_to_all | solution.py:406
  291.6 6.0 %copy-start.3 = (bf16[16,32,128]{2,1,0:T(8,128)(2,1)}, bf16[16,32,128]{2,1,0:T(8,128)(2,1)S(1)}, u32[]{:S(2)}) copy-start(bf16[16,32,128]{2,1,0:T(8,128)(2,1)S(1)} %all-to-all-done.5.parts_ref) | copy-start | bytes 393220
  292.5 25.2 %all-to-all-start.7 = ((f32[256,3,128]{2,1,0:T(4,128)}), f32[256,3,128]{2,1,0:T(4,128)S(1)}, u32[]{:S(2)}, u32[]{:S(2)}) async-start(f32[256,3,128]{2,1,0:T(4,128)} %broadcast_in_dim.8), calls=%async_computation.7 | async-start | bytes 1048576 | tf_op jit(solution)/shard_map/all_to_all | solution.py:419
